TPU v7x, 128 devices: a whole 4x4x4 slice. The times are simulated.
128 devices in a mesh: row: 16 (over z, x), col: 8 (over y, core).
Axes of the slice: x: 4, y: 4, z: 4, core: 2. Of those that a mesh axis runs over, the one named last changes fastest.
Arguments:
- observed: float32 [8192, 8192], P('row', 'col'), may hold values from -6 to 6
- kernel_rows: float32 [31], replicated, may hold values from 0.01 to 0.1
- kernel_cols: float32 [31], replicated, may hold values from 0.01 to 0.1
- air_temp: float32 [8192, 8192], P('row', 'col'), may hold values from -1 to 1
- wind_speed: float32 [8192, 8192], P('row', 'col'), may hold values from 2 to 8
- net_radiation: float32 [8192, 8192], P('row', 'col'), may hold values from 1.5 to 7
- sentinel: bfloat16 [2, 8192, 8192], P(None, 'row', 'col'), may hold values from 0.049804688 to 1
- block_target: int32 [64, 64], P('row', 'col'), may hold values from 0 to 511, as said below
- land_mask: int32 [8192, 8192], P('row', 'col'), may hold values 0 or 1
Outputs:
- sharpened: float32 [8192, 8192], P('row', 'col')
- sensible: float32 [8192, 8192], P('row', 'col')
- latent: float32 [8192, 8192], P('row', 'col')
Inputs may be any that keep to these rules, and one draw needn't show every extreme that they name: Within each column of devices block_target is a bijection onto the blocks of that column; each device sends exactly 2 blocks to each of 16 devices of its column, and none to the others.
All inputs are finite; a program needn't handle non-finite values. No bound on the sum of `land_mask` on one device may be relied on, other than what follows from the above.
Results may differ from a plain program's by a relative error of at most 0.0039.
Values may be sent and summed in bfloat16 or wider, within the bound.
A program may use at most 192 MiB of HBM per device.

v0:
```python
import jax
import jax.numpy as jnp
from jax import lax
from jax.sharding import PartitionSpec as P

BLOCK = 128
TAPS = 31
SWEEPS = 3
ROUNDS = 10
CAPACITY = 2


RHO_CP = 1206.0
STEP_GAIN = 1.5


def with_halo(cells, sides, width):
    for axis, dim in sides:
        count = lax.axis_size(axis)
        ends = count - 1
        head = lax.slice_in_dim(cells, 0, width, axis=dim)
        tail = lax.slice_in_dim(cells, cells.shape[dim] - width, cells.shape[dim], axis=dim)
        cells = jnp.concatenate(
            [
                lax.ppermute(tail, axis, [(i, (i + 1) % count) for i in range(ends)]),
                cells,
                lax.ppermute(head, axis, [((i + 1) % count, i) for i in range(ends)]),
            ],
            axis=dim,
        )
    return cells


def banded(kern, count):
    length = count + TAPS - 1
    line = jnp.concatenate([kern, jnp.zeros((length + 1 - TAPS,), jnp.float32)])
    return jnp.tile(line, count)[: count * length].reshape(count, length)


def pass_rows(band, padded):
    return jnp.dot(
        band, padded, precision=lax.Precision.HIGHEST, preferred_element_type=jnp.float32
    )


def pass_cols(padded, band):
    return jnp.dot(
        padded, band.T, precision=lax.Precision.HIGHEST, preferred_element_type=jnp.float32
    )


def blur(field, band_rows, band_cols):
    half = (TAPS - 1) // 2
    padded = with_halo(field, (("row", 0),), half)
    section = pass_rows(band_rows, padded)
    padded = with_halo(section, (("col", 1),), half)
    return pass_cols(padded, band_cols)


def to_blocks(tile):
    per_r = tile.shape[1] // BLOCK
    per_c = tile.shape[2] // BLOCK
    shaped = tile.reshape(2, per_r, BLOCK, per_c, BLOCK).transpose(1, 3, 0, 2, 4)
    return shaped.reshape(per_r * per_c, 2 * BLOCK * BLOCK)


def from_blocks(blocks, per_r, per_c):
    shaped = blocks.reshape(per_r, per_c, 2, BLOCK, BLOCK).transpose(2, 0, 3, 1, 4)
    return shaped.reshape(2, per_r * BLOCK, per_c * BLOCK)


def route(sentinel, block_target):
    per_r, per_c = block_target.shape
    blocks = to_blocks(sentinel)
    count = blocks.shape[0]
    targets = block_target.reshape(-1)
    owners = lax.axis_size("row")
    device = targets // count
    order = jnp.arange(count, dtype=jnp.int32)
    earlier = (device[:, None] == device[None, :]) & (order[None, :] < order[:, None])
    rank = jnp.sum(earlier.astype(jnp.int32), axis=1)
    slots = device * CAPACITY + rank
    width = owners * CAPACITY
    select = slots[None, :] == jnp.arange(width, dtype=jnp.int32)[:, None]
    outgoing = jnp.dot(select.astype(jnp.bfloat16), blocks, preferred_element_type=jnp.float32)
    outgoing = outgoing.astype(jnp.bfloat16).reshape(owners, CAPACITY, -1)
    labels = jnp.sum(jnp.where(select, (targets % count)[None, :], 0), axis=1)
    labels = jnp.where(jnp.any(select, axis=1), labels, -1).reshape(owners, CAPACITY)
    arrived, tags = (
        lax.all_to_all(outgoing, "row", split_axis=0, concat_axis=0, tiled=True),
        lax.all_to_all(labels, "row", split_axis=0, concat_axis=0, tiled=True),
    )
    placing = tags.reshape(-1)[None, :] == order[:, None]
    landed = jnp.dot(
        placing.astype(jnp.bfloat16), arrived.reshape(width, -1), preferred_element_type=jnp.float32
    )
    landed = landed.astype(jnp.bfloat16)
    return from_blocks(landed, per_r, per_c)


def energy_balance(theta, air, wind, radiation, leaf_raw, cover, land):
    t_rad = 300.0 + 10.0 * theta
    t_air = 300.0 + 10.0 * air
    leaf = 4.0 * leaf_raw
    f_view = 1.0 - jnp.exp(-0.5 * leaf)
    height = 0.1 + 2.0 * cover
    rough = 0.123 * height
    above = 10.0 - 0.67 * height
    log_m = jnp.log(above / rough)
    log_h = jnp.log(7.0 * above / rough)
    net = 100.0 * radiation
    soil_net = net * jnp.exp(-0.45 * leaf)
    ground = 0.35 * soil_net
    celsius = t_air - 273.15
    vapour = 0.6108 * jnp.exp(17.27 * celsius / (celsius + 237.3))
    slope = 4098.0 * vapour / (celsius + 237.3) ** 2
    canopy_h = (net - soil_net) * (1.0 - 1.26 * cover * slope / (slope + 0.066))
    shelter = jnp.exp(-0.5 * leaf)

    def one_round(step, carry):
        zeta, unused_total = carry
        unstable = jnp.minimum(zeta, 0.0)
        stable = jnp.maximum(zeta, 0.0)
        root = (1.0 - 16.0 * unstable) ** 0.25
        psi_m = (
            2.0 * jnp.log((1.0 + root) / 2.0)
            + jnp.log((1.0 + root * root) / 2.0)
            - 2.0 * jnp.arctan(root)
            + jnp.pi / 2.0
            - 5.0 * stable
        )
        psi_h = 2.0 * jnp.log((1.0 + root * root) / 2.0) - 5.0 * stable
        momentum = log_m - psi_m
        friction = 0.41 * wind / momentum
        resist = momentum * (log_h - psi_h) / (0.41 * 0.41 * wind)
        t_canopy = t_air + canopy_h * resist / RHO_CP
        t_soil = (t_rad - f_view * t_canopy) / (1.0 - f_view)
        soil_res = 1.0 / (0.004 + 0.0288 * friction * shelter)
        soil_h = RHO_CP * (t_soil - t_air) / (resist + soil_res)
        total = canopy_h + soil_h
        target = jnp.clip(-0.41 * 9.81 * above * total / (friction**3 * RHO_CP * t_air), -2.0, 0.5)
        return (0.5 * zeta + 0.5 * target, total)

    start = (jnp.zeros_like(theta), jnp.zeros_like(theta))
    zeta, total = lax.fori_loop(0, ROUNDS, one_round, start)
    sensible = jnp.where(land == 1, total / 100.0, 0.0)
    latent = jnp.where(land == 1, (net - ground - total) / 100.0, 0.0)
    return (sensible, latent)


def local(
    observed,
    kernel_rows,
    kernel_cols,
    air_temp,
    wind_speed,
    net_radiation,
    sentinel,
    block_target,
    land_mask,
):
    rows, cols = observed.shape
    row_kernel = kernel_rows / jnp.sum(kernel_rows)
    col_kernel = kernel_cols / jnp.sum(kernel_cols)
    routed = route(sentinel, block_target)
    ahead_rows = banded(row_kernel, rows)
    ahead_cols = banded(col_kernel, cols)
    back_rows = banded(row_kernel[::-1], rows)
    back_cols = banded(col_kernel[::-1], cols)
    estimate = observed
    for sweep in range(SWEEPS):
        misfit = observed - blur(estimate, ahead_rows, ahead_cols)
        estimate = estimate + STEP_GAIN * blur(misfit, back_rows, back_cols)
    sensible, latent = energy_balance(
        estimate,
        air_temp,
        wind_speed,
        net_radiation,
        routed[0].astype(jnp.float32),
        routed[1].astype(jnp.float32),
        land_mask,
    )
    return (estimate, sensible, latent)


def solution(mesh):
    placed = (
        P("row", "col"),
        P(),
        P(),
        P("row", "col"),
        P("row", "col"),
        P("row", "col"),
        P(None, "row", "col"),
        P("row", "col"),
        P("row", "col"),
    )
    return jax.shard_map(
        local,
        mesh=mesh,
        in_specs=placed,
        out_specs=(P("row", "col"), P("row", "col"), P("row", "col")),
        check_vma=False,
    )
```

profile of v0, /device:TPU:24, one launch (start us, length us, event | category | flops | bytes accessed | tf_op | source)
XLA Modules:
  0.0 495.3 jit_solution(13426007780501105572)
XLA Ops:
  32.5 7.4 %tile.41 = f32[1080320]{0:T(1024)} reshape(f32[1024,1055]{1,0:T(8,128)} %tile.40) | data formatting | bytes 8642560 | tf_op jit(solution)/shard_map/tile | solution.py:37
  54.5 11.5 %convolution_subtract_fusion.2 = f32[512,1024]{1,0:T(8,128)S(1)} fusion(f32[512,1024]{1,0:T(8,128)S(1)} %copy-done, f32[512,1054]{1,0:T(8,128)} %concatenate.51, f32[1024,1054]{1,0:T(8,128)} %reshape.181), kind=kOutput, calls=%fused_computation.83 | convolution fusion | flops 6631718912 | bytes 10670080 | tf_op jit(solution)/shard_map/dot_general | solution.py:47
  84.4 7.2 %fusion.12 = f32[512,1024]{1,0:T(8,128)S(1)} fusion(f32[512,542]{1,0:T(8,128)} %reshape.179, f32[15,1024]{1,0:T(8,128)S(1)} %collective-permute-done.5, f32[512,1024]{1,0:T(8,128)} %copy-done.11, f32[15,1024]{1,0:T(8,128)S(1)} %collective-permute-done.4), kind=kOutput, calls=%fused_computation.25 | convolution fusion | flops 3411079168 | bytes 5427200 | tf_op jit(solution)/shard_map/dot_general | solution.py:41
  101.6 7.5 %tile.43 = f32[1080320]{0:T(1024)} reshape(f32[1024,1055]{1,0:T(8,128)} %tile.42) | data formatting | bytes 8642560 | tf_op jit(solution)/shard_map/tile | solution.py:37
  123.6 11.5 %multiply_add_fusion.3 = f32[512,1024]{1,0:T(8,128)S(1)} fusion(f32[512,1024]{1,0:T(8,128)S(1)} %copy-done, f32[512,1054]{1,0:T(8,128)} %concatenate.54, f32[1024,1054]{1,0:T(8,128)} %reshape.182), kind=kOutput, calls=%fused_computation.79 | convolution fusion | flops 6632243200 | bytes 10670080 | tf_op jit(solution)/shard_map/dot_general | solution.py:47
  166.5 11.6 %convolution_subtract_fusion.1 = f32[512,1024]{1,0:T(8,128)S(1)} fusion(f32[512,1024]{1,0:T(8,128)S(1)} %copy-done, f32[512,1054]{1,0:T(8,128)} %concatenate.57, f32[1024,1054]{1,0:T(8,128)} %reshape.181), kind=kOutput, calls=%fused_computation.82 | convolution fusion | flops 6631718912 | bytes 10670080 | tf_op jit(solution)/shard_map/dot_general | solution.py:47
  211.7 11.8 %multiply_add_fusion.2 = f32[512,1024]{1,0:T(8,128)S(1)} fusion(f32[512,1024]{1,0:T(8,128)} %copy-done.4, f32[512,1054]{1,0:T(8,128)} %concatenate.59, f32[1024,1054]{1,0:T(8,128)} %reshape.182), kind=kOutput, calls=%fused_computation.78 | convolution fusion | flops 6632243200 | bytes 10670080 | tf_op jit(solution)/shard_map/dot_general | solution.py:47
  233.5 10.2 %all-to-all-start = ((s32[16,1,2]{2,1,0:T(1,128)}), s32[16,1,2]{2,1,0:T(1,128)S(1)}, u32[]{:S(2)}, u32[]{:S(2)}) async-start(s32[16,1,2]{2,1,0:T(1,128)} %bitcast), calls=%async_computation | async-start | bytes 16384 | tf_op jit(solution)/shard_map/all_to_all | solution.py:91
  275.1 7.4 %all-to-all-start.1 = ((bf16[16,2,32768]{2,1,0:T(2,128)(2,1)}), bf16[16,2,32768]{2,1,0:T(2,128)(2,1)}, u32[]{:S(2)}, u32[]{:S(2)}) async-start(bf16[16,2,32768]{2,1,0:T(2,128)(2,1)} %reshape.186), calls=%async_computation.1 | async-start | bytes 4194304 | tf_op jit(solution)/shard_map/all_to_all | solution.py:90
  282.5 11.6 %convolution_subtract_fusion = f32[512,1024]{1,0:T(8,128)S(1)} fusion(f32[512,1024]{1,0:T(8,128)S(1)} %copy-done, f32[512,1054]{1,0:T(8,128)} %concatenate.61, f32[1024,1054]{1,0:T(8,128)} %reshape.181), kind=kOutput, calls=%fused_computation.81 | convolution fusion | flops 6631718912 | bytes 10670080 | tf_op jit(solution)/shard_map/dot_general | solution.py:47
  299.4 8.9 %collective-permute-done.20 = f32[15,1024]{1,0:T(8,128)S(1)} collective-permute-done((f32[15,1024]{1,0:T(8,128)S(1)}, f32[15,1024]{1,0:T(8,128)S(1)}, u32[]{:S(2)}, u32[]{:S(2)}) %collective-permute-start.20) | collective-permute-done | bytes 61472 | tf_op jit(solution)/shard_map/ppermute | solution.py:25
  315.7 8.0 %collective-permute-start.23 = (f32[512,15]{1,0:T(8,128)S(1)}, f32[512,15]{1,0:T(8,128)S(1)}, u32[]{:S(2)}, u32[]{:S(2)}) collective-permute-start(f32[512,15]{1,0:T(8,128)S(1)} %get-tuple-element.140), channel_id=1, source_target_pairs={{1,0},{2,1},{3,2},{4,3},{5,4},{6,5},{7,6},{9,8},{10,9},{11,10},{12... | collective-permute-start | bytes 92168 | tf_op jit(solution)/shard_map/ppermute | solution.py:27
  334.0 13.0 %multiply_add_fusion = (f32[512,1024]{1,0:T(8,128)S(1)}, f32[512,1024]{1,0:T(8,128)}) fusion(f32[512,1024]{1,0:T(8,128)} %copy-done.3, f32[512,1054]{1,0:T(8,128)} %concatenate.63, f32[1024,1054]{1,0:T(8,128)} %reshape.182), kind=kOutput, calls=%fused_computation.76 | convolution fusion | flops 6633291776 | bytes 12767232 | tf_op jit(solution)/shard_map/dot_general | solution.py:47
  366.6 120.6 %while.14 = (s32[]{:T(128)}, f32[512,1024]{1,0:T(8,128)}, f32[512,1024]{1,0:T(8,128)}, f32[512,1024]{1,0:T(8,128)}, f32[512,1024]{1,0:T(8,128)}, /*index=5*/f32[...) while((s32[]{:T(128)}, f32[512,1024]{1,0:T(8,128)}, ...), condition=%wide.region_6.7_spmd.clone.clone, body=%wide.region_5.6_spmd.clone.sunk.clone | while | flops 27262980 | bytes 25165948 | solution.py:145
  366.8 11.8 %fusion.97 = (f32[512,1024]{1,0:T(8,128)}, f32[512,1024]{1,0:T(8,128)}) fusion(f32[512,1024]{1,0:T(8,128)} %get-tuple-element.309, f32[512,1024]{1,0:T(8,128)} %get-tuple-element.304, f32[512,1024]{1,0:T(8,128)} %get-tuple-element.290, f32[512,1024]{1,0:T(8,128)} %get-tuple-element.307, pred[]{:T(512)S(6)} %compare.28, ...), kind=kLoop, calls=%fused_computation.6.clone.1.clone | loop fusion | flops 27262976 | bytes 25165824 | tf_op jit(solution)/shard_map/while/body/eval_jaxpr/add | solution.py:142
  378.5 12.1 %fusion.97 = (f32[512,1024]{1,0:T(8,128)}, f32[512,1024]{1,0:T(8,128)}) fusion(f32[512,1024]{1,0:T(8,128)} %get-tuple-element.309, f32[512,1024]{1,0:T(8,128)} %get-tuple-element.304, f32[512,1024]{1,0:T(8,128)} %get-tuple-element.290, f32[512,1024]{1,0:T(8,128)} %get-tuple-element.307, pred[]{:T(512)S(6)} %compare.28, ...), kind=kLoop, calls=%fused_computation.6.clone.1.clone | loop fusion | flops 27262976 | bytes 25165824 | tf_op jit(solution)/shard_map/while/body/eval_jaxpr/add | solution.py:142
  390.6 12.1 %fusion.97 = (f32[512,1024]{1,0:T(8,128)}, f32[512,1024]{1,0:T(8,128)}) fusion(f32[512,1024]{1,0:T(8,128)} %get-tuple-element.309, f32[512,1024]{1,0:T(8,128)} %get-tuple-element.304, f32[512,1024]{1,0:T(8,128)} %get-tuple-element.290, f32[512,1024]{1,0:T(8,128)} %get-tuple-element.307, pred[]{:T(512)S(6)} %compare.28, ...), kind=kLoop, calls=%fused_computation.6.clone.1.clone | loop fusion | flops 27262976 | bytes 25165824 | tf_op jit(solution)/shard_map/while/body/eval_jaxpr/add | solution.py:142
  402.7 12.1 %fusion.97 = (f32[512,1024]{1,0:T(8,128)}, f32[512,1024]{1,0:T(8,128)}) fusion(f32[512,1024]{1,0:T(8,128)} %get-tuple-element.309, f32[512,1024]{1,0:T(8,128)} %get-tuple-element.304, f32[512,1024]{1,0:T(8,128)} %get-tuple-element.290, f32[512,1024]{1,0:T(8,128)} %get-tuple-element.307, pred[]{:T(512)S(6)} %compare.28, ...), kind=kLoop, calls=%fused_computation.6.clone.1.clone | loop fusion | flops 27262976 | bytes 25165824 | tf_op jit(solution)/shard_map/while/body/eval_jaxpr/add | solution.py:142
  414.7 12.1 %fusion.97 = (f32[512,1024]{1,0:T(8,128)}, f32[512,1024]{1,0:T(8,128)}) fusion(f32[512,1024]{1,0:T(8,128)} %get-tuple-element.309, f32[512,1024]{1,0:T(8,128)} %get-tuple-element.304, f32[512,1024]{1,0:T(8,128)} %get-tuple-element.290, f32[512,1024]{1,0:T(8,128)} %get-tuple-element.307, pred[]{:T(512)S(6)} %compare.28, ...), kind=kLoop, calls=%fused_computation.6.clone.1.clone | loop fusion | flops 27262976 | bytes 25165824 | tf_op jit(solution)/shard_map/while/body/eval_jaxpr/add | solution.py:142
  426.8 12.1 %fusion.97 = (f32[512,1024]{1,0:T(8,128)}, f32[512,1024]{1,0:T(8,128)}) fusion(f32[512,1024]{1,0:T(8,128)} %get-tuple-element.309, f32[512,1024]{1,0:T(8,128)} %get-tuple-element.304, f32[512,1024]{1,0:T(8,128)} %get-tuple-element.290, f32[512,1024]{1,0:T(8,128)} %get-tuple-element.307, pred[]{:T(512)S(6)} %compare.28, ...), kind=kLoop, calls=%fused_computation.6.clone.1.clone | loop fusion | flops 27262976 | bytes 25165824 | tf_op jit(solution)/shard_map/while/body/eval_jaxpr/add | solution.py:142
  438.9 12.1 %fusion.97 = (f32[512,1024]{1,0:T(8,128)}, f32[512,1024]{1,0:T(8,128)}) fusion(f32[512,1024]{1,0:T(8,128)} %get-tuple-element.309, f32[512,1024]{1,0:T(8,128)} %get-tuple-element.304, f32[512,1024]{1,0:T(8,128)} %get-tuple-element.290, f32[512,1024]{1,0:T(8,128)} %get-tuple-element.307, pred[]{:T(512)S(6)} %compare.28, ...), kind=kLoop, calls=%fused_computation.6.clone.1.clone | loop fusion | flops 27262976 | bytes 25165824 | tf_op jit(solution)/shard_map/while/body/eval_jaxpr/add | solution.py:142
  450.9 12.1 %fusion.97 = (f32[512,1024]{1,0:T(8,128)}, f32[512,1024]{1,0:T(8,128)}) fusion(f32[512,1024]{1,0:T(8,128)} %get-tuple-element.309, f32[512,1024]{1,0:T(8,128)} %get-tuple-element.304, f32[512,1024]{1,0:T(8,128)} %get-tuple-element.290, f32[512,1024]{1,0:T(8,128)} %get-tuple-element.307, pred[]{:T(512)S(6)} %compare.28, ...), kind=kLoop, calls=%fused_computation.6.clone.1.clone | loop fusion | flops 27262976 | bytes 25165824 | tf_op jit(solution)/shard_map/while/body/eval_jaxpr/add | solution.py:142
  463.0 12.1 %fusion.97 = (f32[512,1024]{1,0:T(8,128)}, f32[512,1024]{1,0:T(8,128)}) fusion(f32[512,1024]{1,0:T(8,128)} %get-tuple-element.309, f32[512,1024]{1,0:T(8,128)} %get-tuple-element.304, f32[512,1024]{1,0:T(8,128)} %get-tuple-element.290, f32[512,1024]{1,0:T(8,128)} %get-tuple-element.307, pred[]{:T(512)S(6)} %compare.28, ...), kind=kLoop, calls=%fused_computation.6.clone.1.clone | loop fusion | flops 27262976 | bytes 25165824 | tf_op jit(solution)/shard_map/while/body/eval_jaxpr/add | solution.py:142
  475.1 12.1 %fusion.97 = (f32[512,1024]{1,0:T(8,128)}, f32[512,1024]{1,0:T(8,128)}) fusion(f32[512,1024]{1,0:T(8,128)} %get-tuple-element.309, f32[512,1024]{1,0:T(8,128)} %get-tuple-element.304, f32[512,1024]{1,0:T(8,128)} %get-tuple-element.290, f32[512,1024]{1,0:T(8,128)} %get-tuple-element.307, pred[]{:T(512)S(6)} %compare.28, ...), kind=kLoop, calls=%fused_computation.6.clone.1.clone | loop fusion | flops 27262976 | bytes 25165824 | tf_op jit(solution)/shard_map/while/body/eval_jaxpr/add | solution.py:142
  (159 shorter events, 245.7 us)
Async XLA Ops:
  2.2 14.6 %collective-permute-start = (f32[15,1024]{1,0:T(8,128)}, f32[15,1024]{1,0:T(8,128)S(1)}, u32[]{:S(2)}, u32[]{:S(2)}) collective-permute-start(f32[15,1024]{1,0:T(8,128)} %get-tuple-element.162), channel_id=1, source_target_pairs={{0,8},{8,16},{16,24},{24,32},{32,40},{40,48},{48,56},{56,64},{64,7... | collective-permute-start | bytes 184328 | tf_op jit(solution)/shard_map/ppermute | solution.py:25
  5.6 11.2 %collective-permute-start.1 = (f32[15,1024]{1,0:T(8,128)}, f32[15,1024]{1,0:T(8,128)S(1)}, u32[]{:S(2)}, u32[]{:S(2)}) collective-permute-start(f32[15,1024]{1,0:T(8,128)} %get-tuple-element.163), channel_id=1, source_target_pairs={{8,0},{16,8},{24,16},{32,24},{40,32},{48,40},{56,48},{64,56},{72,6... | collective-permute-start | bytes 184328 | tf_op jit(solution)/shard_map/ppermute | solution.py:27
  24.1 26.0 %collective-permute-start.3 = (f32[512,15]{1,0:T(8,128)}, f32[512,15]{1,0:T(8,128)}, u32[]{:S(2)}, u32[]{:S(2)}) collective-permute-start(f32[512,15]{1,0:T(8,128)} %get-tuple-element.160), channel_id=1, source_target_pairs={{1,0},{2,1},{3,2},{4,3},{5,4},{6,5},{7,6},{9,8},{10,9},{11,10},{12... | collective-permute-start | bytes 92168 | tf_op jit(solution)/shard_map/ppermute | solution.py:27
  26.1 24.1 %collective-permute-start.2 = (f32[512,15]{1,0:T(8,128)}, f32[512,15]{1,0:T(8,128)}, u32[]{:S(2)}, u32[]{:S(2)}) collective-permute-start(f32[512,15]{1,0:T(8,128)} %get-tuple-element.161), channel_id=1, source_target_pairs={{0,1},{1,2},{2,3},{3,4},{4,5},{5,6},{6,7},{8,9},{9,10},{10,11},{11... | collective-permute-start | bytes 92168 | tf_op jit(solution)/shard_map/ppermute | solution.py:25
  68.0 16.4 %collective-permute-start.4 = (f32[15,1024]{1,0:T(8,128)}, f32[15,1024]{1,0:T(8,128)S(1)}, u32[]{:S(2)}, u32[]{:S(2)}) collective-permute-start(f32[15,1024]{1,0:T(8,128)} %get-tuple-element.158), channel_id=1, source_target_pairs={{0,8},{8,16},{16,24},{24,32},{32,40},{40,48},{48,56},{56,64},{64,7... | collective-permute-start | bytes 184328 | tf_op jit(solution)/shard_map/ppermute | solution.py:25
  72.6 11.8 %collective-permute-start.5 = (f32[15,1024]{1,0:T(8,128)}, f32[15,1024]{1,0:T(8,128)S(1)}, u32[]{:S(2)}, u32[]{:S(2)}) collective-permute-start(f32[15,1024]{1,0:T(8,128)} %get-tuple-element.159), channel_id=1, source_target_pairs={{8,0},{16,8},{24,16},{32,24},{40,32},{48,40},{56,48},{64,56},{72,6... | collective-permute-start | bytes 184328 | tf_op jit(solution)/shard_map/ppermute | solution.py:27
  93.8 25.5 %collective-permute-start.7 = (f32[512,15]{1,0:T(8,128)}, f32[512,15]{1,0:T(8,128)}, u32[]{:S(2)}, u32[]{:S(2)}) collective-permute-start(f32[512,15]{1,0:T(8,128)} %get-tuple-element.156), channel_id=1, source_target_pairs={{1,0},{2,1},{3,2},{4,3},{5,4},{6,5},{7,6},{9,8},{10,9},{11,10},{12... | collective-permute-start | bytes 92168 | tf_op jit(solution)/shard_map/ppermute | solution.py:27
  95.9 23.3 %collective-permute-start.6 = (f32[512,15]{1,0:T(8,128)}, f32[512,15]{1,0:T(8,128)}, u32[]{:S(2)}, u32[]{:S(2)}) collective-permute-start(f32[512,15]{1,0:T(8,128)} %get-tuple-element.157), channel_id=1, source_target_pairs={{0,1},{1,2},{2,3},{3,4},{4,5},{5,6},{6,7},{8,9},{9,10},{10,11},{11... | collective-permute-start | bytes 92168 | tf_op jit(solution)/shard_map/ppermute | solution.py:25
  135.2 6.4 %collective-permute-start.8 = (f32[15,1024]{1,0:T(8,128)S(1)}, f32[15,1024]{1,0:T(8,128)S(1)}, u32[]{:S(2)}, u32[]{:S(2)}) collective-permute-start(f32[15,1024]{1,0:T(8,128)S(1)} %get-tuple-element.154), channel_id=1, source_target_pairs={{0,8},{8,16},{16,24},{24,32},{32,40},{40,48},{48,56},{56,64},{64,7... | collective-permute-start | bytes 184328 | tf_op jit(solution)/shard_map/ppermute | solution.py:25
  139.7 6.2 %collective-permute-start.9 = (f32[15,1024]{1,0:T(8,128)S(1)}, f32[15,1024]{1,0:T(8,128)S(1)}, u32[]{:S(2)}, u32[]{:S(2)}) collective-permute-start(f32[15,1024]{1,0:T(8,128)S(1)} %get-tuple-element.155), channel_id=1, source_target_pairs={{8,0},{16,8},{24,16},{32,24},{40,32},{48,40},{56,48},{64,56},{72,6... | collective-permute-start | bytes 184328 | tf_op jit(solution)/shard_map/ppermute | solution.py:27
  154.3 7.8 %collective-permute-start.10 = (f32[512,15]{1,0:T(8,128)S(1)}, f32[512,15]{1,0:T(8,128)}, u32[]{:S(2)}, u32[]{:S(2)}) collective-permute-start(f32[512,15]{1,0:T(8,128)S(1)} %get-tuple-element.153), channel_id=1, source_target_pairs={{0,1},{1,2},{2,3},{3,4},{4,5},{5,6},{6,7},{8,9},{9,10},{10,11},{11... | collective-permute-start | bytes 92168 | tf_op jit(solution)/shard_map/ppermute | solution.py:25
  178.1 6.4 %collective-permute-start.12 = (f32[15,1024]{1,0:T(8,128)S(1)}, f32[15,1024]{1,0:T(8,128)S(1)}, u32[]{:S(2)}, u32[]{:S(2)}) collective-permute-start(f32[15,1024]{1,0:T(8,128)S(1)} %get-tuple-element.150), channel_id=1, source_target_pairs={{0,8},{8,16},{16,24},{24,32},{32,40},{40,48},{48,56},{56,64},{64,7... | collective-permute-start | bytes 184328 | tf_op jit(solution)/shard_map/ppermute | solution.py:25
  182.6 8.3 %collective-permute-start.13 = (f32[15,1024]{1,0:T(8,128)S(1)}, f32[15,1024]{1,0:T(8,128)S(1)}, u32[]{:S(2)}, u32[]{:S(2)}) collective-permute-start(f32[15,1024]{1,0:T(8,128)S(1)} %get-tuple-element.151), channel_id=1, source_target_pairs={{8,0},{16,8},{24,16},{32,24},{40,32},{48,40},{56,48},{64,56},{72,6... | collective-permute-start | bytes 184328 | tf_op jit(solution)/shard_map/ppermute | solution.py:27
  199.5 7.8 %collective-permute-start.14 = (f32[512,15]{1,0:T(8,128)S(1)}, f32[512,15]{1,0:T(8,128)}, u32[]{:S(2)}, u32[]{:S(2)}) collective-permute-start(f32[512,15]{1,0:T(8,128)S(1)} %get-tuple-element.149), channel_id=1, source_target_pairs={{0,1},{1,2},{2,3},{3,4},{4,5},{5,6},{6,7},{8,9},{9,10},{10,11},{11... | collective-permute-start | bytes 92168 | tf_op jit(solution)/shard_map/ppermute | solution.py:25
  225.5 26.5 %collective-permute-start.16 = (f32[15,1024]{1,0:T(8,128)}, f32[15,1024]{1,0:T(8,128)S(1)}, u32[]{:S(2)}, u32[]{:S(2)}) collective-permute-start(f32[15,1024]{1,0:T(8,128)} %get-tuple-element.146), channel_id=1, source_target_pairs={{0,8},{8,16},{16,24},{24,32},{32,40},{40,48},{48,56},{56,64},{64,7... | collective-permute-start | bytes 184328 | tf_op jit(solution)/shard_map/ppermute | solution.py:25
  231.5 20.4 %collective-permute-start.17 = (f32[15,1024]{1,0:T(8,128)}, f32[15,1024]{1,0:T(8,128)S(1)}, u32[]{:S(2)}, u32[]{:S(2)}) collective-permute-start(f32[15,1024]{1,0:T(8,128)} %get-tuple-element.147), channel_id=1, source_target_pairs={{8,0},{16,8},{24,16},{32,24},{40,32},{48,40},{56,48},{64,56},{72,6... | collective-permute-start | bytes 184328 | tf_op jit(solution)/shard_map/ppermute | solution.py:27
  233.5 41.6 %all-to-all-start = ((s32[16,1,2]{2,1,0:T(1,128)}), s32[16,1,2]{2,1,0:T(1,128)S(1)}, u32[]{:S(2)}, u32[]{:S(2)}) async-start(s32[16,1,2]{2,1,0:T(1,128)} %bitcast), calls=%async_computation | async-start | bytes 16384 | tf_op jit(solution)/shard_map/all_to_all | solution.py:91
  260.4 10.8 %collective-permute-start.19 = (f32[512,15]{1,0:T(8,128)S(1)}, f32[512,15]{1,0:T(8,128)S(1)}, u32[]{:S(2)}, u32[]{:S(2)}) collective-permute-start(f32[512,15]{1,0:T(8,128)S(1)} %get-tuple-element.144), channel_id=1, source_target_pairs={{1,0},{2,1},{3,2},{4,3},{5,4},{6,5},{7,6},{9,8},{10,9},{11,10},{12... | collective-permute-start | bytes 92168 | tf_op jit(solution)/shard_map/ppermute | solution.py:27
  262.3 8.9 %collective-permute-start.18 = (f32[512,15]{1,0:T(8,128)S(1)}, f32[512,15]{1,0:T(8,128)S(1)}, u32[]{:S(2)}, u32[]{:S(2)}) collective-permute-start(f32[512,15]{1,0:T(8,128)S(1)} %get-tuple-element.145), channel_id=1, source_target_pairs={{0,1},{1,2},{2,3},{3,4},{4,5},{5,6},{6,7},{8,9},{9,10},{10,11},{11... | collective-permute-start | bytes 92168 | tf_op jit(solution)/shard_map/ppermute | solution.py:25
  275.1 71.8 %all-to-all-start.1 = ((bf16[16,2,32768]{2,1,0:T(2,128)(2,1)}), bf16[16,2,32768]{2,1,0:T(2,128)(2,1)}, u32[]{:S(2)}, u32[]{:S(2)}) async-start(bf16[16,2,32768]{2,1,0:T(2,128)(2,1)} %reshape.186), calls=%async_computation.1 | async-start | bytes 4194304 | tf_op jit(solution)/shard_map/all_to_all | solution.py:90
  294.1 14.1 %collective-permute-start.20 = (f32[15,1024]{1,0:T(8,128)S(1)}, f32[15,1024]{1,0:T(8,128)S(1)}, u32[]{:S(2)}, u32[]{:S(2)}) collective-permute-start(f32[15,1024]{1,0:T(8,128)S(1)} %get-tuple-element.142), channel_id=1, source_target_pairs={{0,8},{8,16},{16,24},{24,32},{32,40},{40,48},{48,56},{56,64},{64,7... | collective-permute-start | bytes 184328 | tf_op jit(solution)/shard_map/ppermute | solution.py:25
  297.9 12.5 %collective-permute-start.21 = (f32[15,1024]{1,0:T(8,128)S(1)}, f32[15,1024]{1,0:T(8,128)S(1)}, u32[]{:S(2)}, u32[]{:S(2)}) collective-permute-start(f32[15,1024]{1,0:T(8,128)S(1)} %get-tuple-element.143), channel_id=1, source_target_pairs={{8,0},{16,8},{24,16},{32,24},{40,32},{48,40},{56,48},{64,56},{72,6... | collective-permute-start | bytes 184328 | tf_op jit(solution)/shard_map/ppermute | solution.py:27
  315.7 11.8 %collective-permute-start.23 = (f32[512,15]{1,0:T(8,128)S(1)}, f32[512,15]{1,0:T(8,128)S(1)}, u32[]{:S(2)}, u32[]{:S(2)}) collective-permute-start(f32[512,15]{1,0:T(8,128)S(1)} %get-tuple-element.140), channel_id=1, source_target_pairs={{1,0},{2,1},{3,2},{4,3},{5,4},{6,5},{7,6},{9,8},{10,9},{11,10},{12... | collective-permute-start | bytes 92168 | tf_op jit(solution)/shard_map/ppermute | solution.py:27
  323.7 7.7 %collective-permute-start.22 = (f32[512,15]{1,0:T(8,128)S(1)}, f32[512,15]{1,0:T(8,128)S(1)}, u32[]{:S(2)}, u32[]{:S(2)}) collective-permute-start(f32[512,15]{1,0:T(8,128)S(1)} %get-tuple-element.141), channel_id=1, source_target_pairs={{0,1},{1,2},{2,3},{3,4},{4,5},{5,6},{6,7},{8,9},{9,10},{10,11},{11... | collective-permute-start | bytes 92168 | tf_op jit(solution)/shard_map/ppermute | solution.py:25
  (20 other events, 158.5 us)
where the time goes:
time: 502 us; the launch traced here: 495 us
  other arithmetic  144 us (29%)
  local copies, waits for them, and re-layouts  116 us (23%)
  matrix products  110 us (22%)
  starting transfers between devices  87.7 us (17%)
  waiting for transfers between devices  35.9 us (7%)
    add x10, other arithmetic, one_round(): return (0.5 * zeta + 0.5 * target, total)  120 us
    dot_general x6, matrix products, pass_cols(): jnp.dot(padded, band.T, precision=lax.Precision.HIGHEST, preferred_elemen...  71 us
    ppermute x12, starting transfers between devices, with_halo(): lax.ppermute(tail, axis, [(i, (i + 1) % count) for i in range(ends)])  43.8 us
    dot_general x6, matrix products, pass_rows(): jnp.dot(band, padded, precision=lax.Precision.HIGHEST, preferred_element_...  34.8 us
    ppermute x12, starting transfers between devices, with_halo(): lax.ppermute(head, axis, [((i + 1) % count, i) for i in range(ends)])  26.3 us
    another operation x8, local copies, waits for them, and re-layouts, banded(): return jnp.tile(line, count)[:count * length].reshape(count, length)  25.5 us
    concatenate x6, local copies, waits for them, and re-layouts, with_halo(): jnp.concatenate([lax.ppermute(tail, axis, [(i, (i + 1) % count) for i in...  24 us
    ppermute x12, waiting for transfers between devices, with_halo(): lax.ppermute(tail, axis, [(i, (i + 1) % count) for i in range(ends)])  21.1 us
  transfers between devices with their start and end apart: 26, of which 12 were waited for; matrix products, arithmetic and copies ran while one was open for 25% of the time, Pallas kernels for 0%

commit v1 on v0

v1 whole, which is shorter than its diff:
```python
import functools
import math

import jax
import jax.numpy as jnp
from jax import lax
from jax.experimental import pallas as pl
from jax.experimental.pallas import tpu as pltpu
from jax.sharding import PartitionSpec as P

BLOCK = 128
RHO_CP = 1206.0
KARMAN = 0.41
ROUNDS = 10
HALF = 5.0 / 32.0
PSI_M = (0.3186391636950537, 0.2200187838733655, 0.02620018653896533, -0.0003221872048960583,
    -0.00019792193220718868, 1.335036373641197e-05, 2.0235608468337185e-06)
BASE = math.log(7.0) / 2.0 + math.log(2.0 * math.sqrt(HALF))
FIXED = 12


def rcp(v):
    return pl.reciprocal(v, approx=True)


def prepare(theta, air, wind, radiation, leaf_raw, cover):
    t_rad = 300.0 + 10.0 * theta
    t_air = 300.0 + 10.0 * air
    leaf = 4.0 * leaf_raw
    e = jnp.exp(-0.5 * leaf)
    f_view = 1.0 - e
    bare = 1.0 - f_view
    height = 0.1 + 2.0 * cover
    rough = 0.123 * height
    above = 10.0 - 0.67 * height
    log_m = 0.5 * jnp.log(above / rough)
    log_h = 0.5 * jnp.log(7.0 * above / rough)
    net = 100.0 * radiation
    soil_net = net * jnp.exp(-0.45 * leaf)
    ground = 0.35 * soil_net
    celsius = t_air - 273.15
    vapour = 0.6108 * jnp.exp(17.27 * celsius / (celsius + 237.3))
    slope = 4098.0 * vapour / ((celsius + 237.3) * (celsius + 237.3))
    canopy = (net - soil_net) * (1.0 - 1.26 * cover * slope / (slope + 0.066))
    k2w = KARMAN * KARMAN * wind
    beta = (3.6 * KARMAN) * wind * e
    iota = k2w * (1.0 / (0.004 * 4.0))
    c3k = (16.0 * HALF * 9.81 * 4.0 / (RHO_CP * KARMAN * KARMAN)) * above * rcp(wind * wind * wind * t_air)
    held = (log_m + BASE, beta, iota, canopy, c3k, 0.25 * k2w, t_air, t_rad, f_view, bare, net - ground)
    return held, log_m, log_h


def flux(m, h, beta, iota, canopy, c3k, quarter, t_air, t_rad, f_view, bare):
    t_canopy = t_air + canopy * ((m * h) / quarter) / RHO_CP
    t_soil = (t_rad - f_view * t_canopy) / bare
    shifted = m + beta
    return canopy * m + (RHO_CP * (t_soil - t_air)) * (quarter * shifted) * rcp(h * shifted + iota)


def advance(zeta, m, h, *held):
    return 0.5 * zeta + jnp.clip((held[3] * (m * m)) * flux(m, h, *held), -4.0 * HALF, 16.0 * HALF)


def stability(zeta, lm):
    base = lm - jnp.minimum(zeta, 0.0)
    a = jnp.maximum(zeta, 0.0) + HALF
    w = jnp.log(a)
    poly = PSI_M[-1]
    for c in PSI_M[-2:0:-1]:
        poly = poly * w + c
    poly = poly * w + (PSI_M[0] + BASE)
    return base - poly, base - jnp.log(a * lax.rsqrt(a) + math.sqrt(HALF))


def energy_kernel(cfg, place, arrived, theta, air, wind, rad, land, out, sens, lat, held):
    rows, sub, width, unroll, pre = cfg
    step = pl.program_id(0)
    band = theta.shape[0]
    per = BLOCK // band
    cols = theta.shape[1] // BLOCK
    out[...] = theta[...]

    def where(j, r, n):
        return pl.ds(pl.multiple_of(r, n), n), pl.ds(pl.multiple_of(j * BLOCK, BLOCK), BLOCK)

    def fill(t, carry):
        j = t // (band // pre)
        r = (t % (band // pre)) * pre
        slot = place[0, (step // per) * cols + j]
        at = where(j, r, pre)
        inner = pl.multiple_of((slot % 2) * (2 * BLOCK) + (step % per) * band + r, pre)
        leaf = arrived[slot // 2, pl.ds(inner, pre), :].astype(jnp.float32)
        cover = arrived[slot // 2, pl.ds(inner + BLOCK, pre), :].astype(jnp.float32)
        values, m, h = prepare(theta[at], air[at], wind[at], rad[at], leaf, cover)
        for n, v in enumerate(values):
            held[(n, *at)] = v
        held[(11, *at)] = jnp.clip((values[4] * (m * m)) * flux(m, h, *values[1:10]), -4.0 * HALF, 16.0 * HALF)
        return carry

    lax.fori_loop(0, cols * (band // pre), fill, 0)

    def col(t, carry):
        pieces = []
        for q in range(width):
            tt = t * width + q
            j = tt // (band // rows)
            r = (tt % (band // rows)) * rows
            for s in range(rows // sub):
                pieces.append(where(j, r + s * sub, sub))

        def one(i, zetas):
            new = []
            for at, zeta in zip(pieces, zetas):
                m, h = stability(zeta, held[(0, *at)])
                new.append(advance(zeta, m, h, *(held[(n, *at)] for n in range(1, 10))))
            return tuple(new)

        zetas = lax.fori_loop(0, ROUNDS - 2, one, tuple(held[(11, *at)] for at in pieces), unroll=unroll)
        for at, zeta in zip(pieces, zetas):
            m, h = stability(zeta, held[(0, *at)])
            total = flux(m, h, *(held[(n, *at)] for n in range(1, 10))) / m
            keep = land[at] == 1
            sens[at] = jnp.where(keep, 0.01 * total, 0.0)
            lat[at] = jnp.where(keep, 0.01 * (held[(10, *at)] - total), 0.0)
        return carry

    lax.fori_loop(0, cols * (band // rows) // width, col, 0)


def energy(place, arrived, theta, air, wind, rad, land, band=128, rows=128, sub=16, width=1, unroll=4, pre=64):
    shape = theta.shape
    spec = pl.BlockSpec((band, shape[1]), lambda i, place: (i, 0))
    return pl.pallas_call(
        functools.partial(energy_kernel, (rows, sub, width, unroll, pre)),
        grid_spec=pltpu.PrefetchScalarGridSpec(
            num_scalar_prefetch=1,
            grid=(shape[0] // band,),
            in_specs=[pl.BlockSpec(arrived.shape, lambda i, place: (0, 0, 0))] + [spec] * 5,
            out_specs=[spec] * 3,
            scratch_shapes=[pltpu.VMEM((FIXED, band, shape[1]), jnp.float32)],
        ),
        out_shape=[jax.ShapeDtypeStruct(shape, jnp.float32)] * 3,
        compiler_params=pltpu.CompilerParams(vmem_limit_bytes=48 << 20),
        name="energy",
    )(place, arrived, theta, air, wind, rad, land)


TAPS = 31
SPAN = TAPS // 2
STEP_GAIN = 1.5
MESH = pl.DeviceIdType.MESH
FRAME = 96
EDGE = 128
TAIL = 16
WINDOW = 256
TALL = 192


def split(value):
    first = value.astype(jnp.bfloat16)
    rest = value - first.astype(jnp.float32)
    second = rest.astype(jnp.bfloat16)
    return first, second, (rest - second.astype(jnp.float32)).astype(jnp.bfloat16)


def mul(a, b):
    return jnp.dot(a, b, preferred_element_type=jnp.float32)


def precise(a, b):
    a1, a2, a3 = split(a)
    b1, b2, b3 = split(b)
    return mul(a1, b1) + ((mul(a2, b1) + mul(a1, b2)) + (mul(a2, b2) + (mul(a3, b1) + mul(a1, b3))))


def taps_matrix(out, taps, rows, cols, offset, sign):
    total = taps[0]
    for t in range(1, TAPS):
        total = total + taps[t]
    part = 64

    def fill(n, carry):
        at = pl.multiple_of(n * part, part)
        i = lax.broadcasted_iota(jnp.int32, (part, cols), 0) + at
        j = lax.broadcasted_iota(jnp.int32, (part, cols), 1)
        which = offset + sign * (i - j)
        acc = jnp.zeros((part, cols), jnp.float32)
        for t in range(TAPS):
            acc = jnp.where(which == t, taps[t], acc)
        out[pl.ds(at, part), :cols] = acc / jnp.full((part, cols), total, jnp.float32)
        return carry

    lax.fori_loop(0, rows // part, fill, 0)


def inside(shape, dim, first, size):
    at = lax.broadcasted_iota(jnp.int32, shape, dim) + first
    return (at >= 0) & (at < size)


def sweep_kernel(
    n_row, n_col, krow_any, kcol_any, target_any, observed, sentinel, sharp, arrived, place,
    krow, kcol, target, pool, outbox, wide, flat, mid, midb, state, nudge, first, second,
    row_g, row_b, col_g, col_b, labels, halo_send, halo_recv, block_send, block_recv, local_sem,
):
    row, col = lax.axis_index("row"), lax.axis_index("col")
    tile_rows, tile_cols = observed.shape
    per_c = tile_cols // BLOCK
    blocks = (tile_rows // BLOCK) * per_c
    rows, cols = tile_rows + 2 * FRAME, tile_cols + 2 * EDGE
    row0, col0 = row * tile_rows, col * tile_cols
    scene_rows, scene_cols = n_row * tile_rows, n_col * tile_cols
    sides = [(dr, dc) for dr in (-1, 0, 1) for dc in (-1, 0, 1) if (dr, dc) != (0, 0)]

    def shifted(dr, dc):
        return lax.rem(row + (dr + n_row), n_row), lax.rem(col + (dc + n_col), n_col)

    barrier = pltpu.get_barrier_semaphore()
    for dr, dc in sides:
        if dc != 0:
            pl.semaphore_signal(barrier, inc=1, device_id=shifted(dr, dc), device_id_type=MESH)

    def greet(k, carry):
        pl.semaphore_signal(barrier, inc=1, device_id=(lax.rem(row + k, n_row), col), device_id_type=MESH)
        return carry

    lax.fori_loop(1, n_row, greet, 0)
    for n, (source, held) in enumerate(((target_any, target), (krow_any, krow), (kcol_any, kcol))):
        pltpu.make_async_copy(source, held, local_sem.at[3 + n]).start()

    def gather(n, carry):
        at = (pl.ds(pl.multiple_of((n // per_c) * BLOCK, BLOCK), BLOCK), pl.ds(pl.multiple_of((n % per_c) * BLOCK, BLOCK), BLOCK))
        for ch in range(2):
            pltpu.make_async_copy(sentinel.at[(ch, *at)], pool.at[n, pl.ds(ch * BLOCK, BLOCK), :], local_sem.at[6]).start()
        return carry

    lax.fori_loop(0, blocks, gather, 0)
    own = pltpu.make_async_copy(observed, wide.at[pl.ds(FRAME, tile_rows), pl.ds(EDGE, tile_cols)], local_sem.at[0])
    own.start()
    pl.semaphore_wait(barrier, 6 + n_row - 1)

    def span(d, length, frame):
        if d == 0:
            return pl.ds(0, length), pl.ds(frame, length)
        if d > 0:
            return pl.ds(length - frame, frame), pl.ds(0, frame)
        return pl.ds(0, frame), pl.ds(frame + length, frame)

    halos = []
    for n, (dr, dc) in enumerate(sides):
        src_r, dst_r = span(dr, tile_rows, FRAME)
        src_c, dst_c = span(dc, tile_cols, EDGE)
        halos.append(pltpu.make_async_remote_copy(
            src_ref=observed.at[src_r, src_c],
            dst_ref=wide.at[dst_r, dst_c],
            send_sem=halo_send.at[n],
            recv_sem=halo_recv.at[n],
            device_id=shifted(dr, dc),
            device_id_type=MESH,
        ))
    for halo in halos:
        halo.start()

    pltpu.make_async_copy(target_any, target, local_sem.at[3]).wait()
    pltpu.make_async_copy(pool, pool, local_sem.at[6]).wait()

    def pack(k):
        dest = lax.rem(row + k, n_row)

        def scan(n, found):
            low, high, low_tag, high_tag = found
            aim = target[n // per_c, n % per_c]
            here = aim // blocks == dest
            earlier = here & (low > n)
            return (
                jnp.where(earlier, n, low), jnp.where(here, n, high),
                jnp.where(earlier, aim, low_tag), jnp.where(here, aim, high_tag),
            )

        start = (jnp.int32(blocks - 1), jnp.int32(0), jnp.int32(0), jnp.int32(0))
        low, high, low_tag, high_tag = lax.fori_loop(0, blocks, scan, start, unroll=8)
        line = lax.broadcasted_iota(jnp.int32, (TAIL, BLOCK), 0)
        tags = jnp.zeros((TAIL, BLOCK), jnp.float32)
        for which, (n, tag) in enumerate(((low, low_tag), (high, high_tag))):
            outbox[k, pl.ds(2 * which * BLOCK, 2 * BLOCK), :] = pool[n]
            tags = jnp.where(line == which, lax.rem(tag, blocks).astype(jnp.float32), tags)
        outbox[k, pl.ds(4 * BLOCK, TAIL), :] = tags.astype(jnp.bfloat16)

    def parcel(k):
        return pltpu.make_async_remote_copy(
            src_ref=outbox.at[k],
            dst_ref=arrived.at[row],
            send_sem=block_send.at[k],
            recv_sem=block_recv.at[k],
            device_id=(lax.rem(row + k, n_row), col),
            device_id_type=MESH,
        )

    def post(k, carry):
        pack(k)
        parcel(k).start()
        return carry

    lax.fori_loop(1, n_row, post, 0)
    pack(0)
    kept = pltpu.make_async_copy(outbox.at[0], arrived.at[row], local_sem.at[1])
    kept.start()

    for n, (source, held) in enumerate(((krow_any, krow), (kcol_any, kcol))):
        pltpu.make_async_copy(source, held, local_sem.at[4 + n]).wait()
    half = WINDOW // 4
    taps_matrix(first, krow, TALL, WINDOW, 47, 1)
    taps_matrix(second, krow, WINDOW, WINDOW, SPAN, -1)
    row_b[:TALL, :], row_b[TALL:2 * TALL, :], row_b[2 * TALL:, :] = split(first[:TALL, :])
    starts = (-64, -32, 0, 416, 352, 384)
    for n, start in enumerate((None, *starts)):
        left = first[:TALL, :]
        if start is not None:
            left = jnp.where(inside((TALL, WINDOW), 1, row0 + (start - FRAME // 3), scene_rows), left, 0.0)
        row_g[n, :TALL, :], row_g[n, TALL:2 * TALL, :], row_g[n, 2 * TALL:, :] = split(precise(left, second[...]))
    taps_matrix(first, kcol, WINDOW, BLOCK, half + SPAN, -1)
    taps_matrix(second, kcol, WINDOW, WINDOW, SPAN, 1)
    col_b[:, :BLOCK], col_b[:, BLOCK:2 * BLOCK], col_b[:, 2 * BLOCK:] = split(first[:, :BLOCK])
    for n, start in enumerate((None, 0, tile_cols - BLOCK)):
        right = first[:, :BLOCK]
        if start is not None:
            right = jnp.where(inside((WINDOW, BLOCK), 0, col0 + (start - half), scene_cols), right, 0.0)
        col_g[n, :, :BLOCK], col_g[n, :, BLOCK:2 * BLOCK], col_g[n, :, 2 * BLOCK:] = split(precise(second[...], right))
    for ref in (mid, midb):
        for n in range(3):
            ref[n, pl.ds(rows, 32), :] = jnp.zeros((32, cols), jnp.bfloat16)

    own.wait()
    for halo in halos:
        halo.wait()

    def flatten(source, height, masked):
        part = 64

        def piece(n, carry):
            at = pl.ds(pl.multiple_of(n * part, part), part)
            lane = lax.broadcasted_iota(jnp.int32, (part, BLOCK), 1)
            before = jnp.zeros((part, BLOCK), jnp.float32)
            for t in range(cols // BLOCK + 1):
                if t < cols // BLOCK:
                    value = source[at, pl.ds(t * BLOCK, BLOCK)]
                    if masked:
                        value = jnp.where(
                            inside((part, BLOCK), 0, row0 + (n * part - FRAME), scene_rows)
                            & inside((part, BLOCK), 1, col0 + (t * BLOCK - EDGE), scene_cols), value, 0.0)
                        source[at, pl.ds(t * BLOCK, BLOCK)] = value
                    turned = pltpu.roll(value, BLOCK // 2, 1)
                else:
                    turned = jnp.zeros((part, BLOCK), jnp.float32)
                for q, part_q in enumerate(split(jnp.where(lane < BLOCK // 2, before, turned))):
                    flat[q, at, pl.ds(t * BLOCK, BLOCK)] = part_q
                before = turned
            return carry

        lax.fori_loop(0, height // part, piece, 0)

    def along_cols(height, begin, end, both):
        def block(j, carry):
            at = pl.ds(pl.multiple_of(j * BLOCK, BLOCK), WINDOW)
            put = (pl.ds(0, height), pl.ds(pl.multiple_of(j * BLOCK, BLOCK), BLOCK))
            kind = jnp.where(j == 1, 1, jnp.where(j == per_c, 2, 0))
            x1, x2, x3 = (flat[q, pl.ds(0, height), at] for q in range(3))

            def apply(weights, to):
                got = mul(x2, weights[:, :2 * BLOCK]) + mul(x1, weights[:, :2 * BLOCK])
                small = mul(x3, weights[:, :BLOCK]) + mul(x1, weights[:, 2 * BLOCK:])
                for q, part_q in enumerate(split(got[:, :BLOCK] + (got[:, BLOCK:] + small))):
                    to[(q, *put)] = part_q

            apply(col_g[kind], mid)
            if both:
                apply(col_b[...], midb)
            return carry

        lax.fori_loop(begin, end, block, 0)

    def along_rows(weights, source, at, length):
        top = mul(weights, source[(0, *at)])
        more = mul(weights[:2 * TALL, :], source[(1, *at)])
        least = mul(weights[:TALL, :], source[(2, *at)])
        small = (top[2 * TALL:2 * TALL + length] + more[TALL:TALL + length]) + least[:length]
        return top[:length] + ((top[TALL:TALL + length] + more[:length]) + small)

    def update(start, sizes, kinds, before, shift, height, after, begin, end):
        offset = 0
        for size, kind in zip(sizes, kinds):
            def strip(n, carry, offset=offset, size=size, kind=kind):
                across = pl.ds(pl.multiple_of(n * WINDOW, WINDOW) + begin, WINDOW)
                at = (pl.ds(offset, WINDOW), across)
                blurred = along_rows(row_g[kind], mid, at, size)
                if start == -64:
                    extra = along_rows(row_b[...], midb, at, size)
                    nudge[pl.ds(offset, size), across] = extra
                else:
                    extra = nudge[pl.ds(offset + start + 64, size), across]
                value = before[pl.ds(offset + shift, size), across] + STEP_GAIN * (extra - blurred)
                if start == 0:
                    after[pl.ds(offset, size), pl.ds(pl.multiple_of(n * WINDOW, WINDOW), WINDOW)] = value
                else:
                    after[pl.ds(offset, size), across] = jnp.where(
                        inside((size, WINDOW), 0, row0 + (start + offset), scene_rows)
                        & inside((size, WINDOW), 1, col0 + (n * WINDOW - EDGE), scene_cols), value, 0.0)
                return carry

            lax.fori_loop(0, (end - begin) // WINDOW, strip, 0)
            offset += size

    flatten(wide, rows, True)
    along_cols(rows, 0, cols // BLOCK, True)
    update(-64, (160, 160, 160, 160), (1, 0, 0, 4), wide, 32, rows - 64, state, 0, cols)
    flatten(state, rows - 64, False)
    along_cols(rows - 64, 0, cols // BLOCK, False)
    update(-32, (192, 192, 192), (2, 0, 5), state, 32, rows - 128, wide, 0, cols)
    flatten(wide, rows - 128, False)
    along_cols(rows - 128, 1, 1 + per_c, False)
    update(0, (192, 192, 128), (3, 0, 6), wide, 32, tile_rows, sharp, EDGE, EDGE + tile_cols)

    kept.wait()

    def collect(k, carry):
        parcel(k).wait()
        return carry

    lax.fori_loop(1, n_row, collect, 0)
    fetch = pltpu.make_async_copy(arrived.at[:, pl.ds(4 * BLOCK, TAIL), :], labels, local_sem.at[2])
    fetch.start()
    fetch.wait()
    lane = lax.broadcasted_iota(jnp.int32, (1, BLOCK), 1)
    found = jnp.zeros((1, BLOCK), jnp.int32)
    for r in range(n_row):
        for which in range(2):
            tag = labels[r][which:which + 1, :].astype(jnp.float32).astype(jnp.int32)
            found = jnp.where(tag == lane, 2 * r + which, found)
    place[...] = found


def sweeps(n_row, n_col, krow, kcol, target, observed, sentinel):
    tile_rows, tile_cols = observed.shape
    rows, cols = tile_rows + 2 * FRAME, tile_cols + 2 * EDGE
    f32, b16 = jnp.float32, jnp.bfloat16
    vmem = pl.BlockSpec(memory_space=pltpu.VMEM)
    any_ = pl.BlockSpec(memory_space=pl.ANY)
    parcel = 4 * BLOCK + TAIL
    return pl.pallas_call(
        functools.partial(sweep_kernel, n_row, n_col),
        in_specs=[any_] * 5,
        out_specs=[vmem, any_, vmem],
        out_shape=[
            jax.ShapeDtypeStruct((tile_rows, tile_cols), f32),
            jax.ShapeDtypeStruct((n_row, parcel, BLOCK), b16),
            jax.ShapeDtypeStruct((1, BLOCK), jnp.int32),
        ],
        scratch_shapes=[
            pltpu.SMEM(krow.shape, f32),
            pltpu.SMEM(kcol.shape, f32),
            pltpu.SMEM(target.shape, jnp.int32),
            pltpu.VMEM((target.size, 2 * BLOCK, BLOCK), b16),
            pltpu.VMEM((n_row, parcel, BLOCK), b16),
            pltpu.VMEM((rows, cols), f32),
            pltpu.VMEM((3, rows, cols + BLOCK), b16),
            pltpu.VMEM((3, rows + 32, cols), b16),
            pltpu.VMEM((3, rows + 32, cols), b16),
            pltpu.VMEM((rows - 64, cols), f32),
            pltpu.VMEM((rows - 64, cols), f32),
            pltpu.VMEM((WINDOW, WINDOW), f32),
            pltpu.VMEM((WINDOW, WINDOW), f32),
            pltpu.VMEM((7, 3 * TALL, WINDOW), b16),
            pltpu.VMEM((3 * TALL, WINDOW), b16),
            pltpu.VMEM((3, WINDOW, 3 * BLOCK), b16),
            pltpu.VMEM((WINDOW, 3 * BLOCK), b16),
            pltpu.VMEM((n_row, TAIL, BLOCK), b16),
            pltpu.SemaphoreType.DMA((8,)),
            pltpu.SemaphoreType.DMA((8,)),
            pltpu.SemaphoreType.DMA((n_row,)),
            pltpu.SemaphoreType.DMA((n_row,)),
            pltpu.SemaphoreType.DMA((7,)),
        ],
        compiler_params=pltpu.CompilerParams(collective_id=0, has_side_effects=True, vmem_limit_bytes=48 << 20),
        name="sweeps",
    )(krow, kcol, target, observed, sentinel)


def local(n_row, n_col, observed, kernel_rows, kernel_cols, air_temp, wind_speed, net_radiation, sentinel, block_target, land_mask):
    theta, arrived, place = sweeps(n_row, n_col, kernel_rows, kernel_cols, block_target, observed, sentinel)
    return energy(place, arrived, theta, air_temp, wind_speed, net_radiation, land_mask)


def solution(mesh):
    tile = P("row", "col")
    return jax.shard_map(
        functools.partial(local, mesh.shape["row"], mesh.shape["col"]),
        mesh=mesh,
        in_specs=(tile, P(), P(), tile, tile, tile, P(None, "row", "col"), tile, tile),
        out_specs=(tile, tile, tile),
        check_vma=False,
    )
```

time: 502 us -> 119 us (0.24); the launches traced: 495 us -> 117 us
  other arithmetic: 144 us -> 0 us
  Pallas kernels: 0 us -> 113 us
  local copies, waits for them, and re-layouts: 116 us -> 3.73 us
  matrix products: 110 us -> 0 us
  starting transfers between devices: 87.7 us -> 0 us
  waiting for transfers between devices: 35.9 us -> 0 us
    add x12 -> x0, other arithmetic: 124 us -> none  [the longest x10 120 us: one_round(): return (0.5 * zeta + 0.5 * target, total)]
    pallas_call x0 -> x2, Pallas kernels: none -> 113 us  [the longest x1 65.3 us: sweeps(): pl.pallas_call(functools.partial(sweep_kernel, n_row, n_col), in_specs=[a...]
    dot_general x14 -> x0, matrix products: 110 us -> none  [the longest x6 71 us: pass_cols(): jnp.dot(padded, band.T, precision=lax.Precision.HIGHEST, preferred_elemen...]
    ppermute x24 -> x0, starting transfers between devices: 70.1 us -> none  [the longest x12 43.8 us: with_halo(): lax.ppermute(tail, axis, [(i, (i + 1) % count) for i in range(ends)])]
    ppermute x24 -> x0, waiting for transfers between devices: 35.9 us -> none  [the longest x12 21.1 us: with_halo(): lax.ppermute(tail, axis, [(i, (i + 1) % count) for i in range(ends)])]
    reshape x10 -> x0, local copies, waits for them, and re-layouts: 33.2 us -> none  [the longest x4 18.5 us: banded(): return jnp.tile(line, count)[:count * length].reshape(count, length)]
    another operation x10 -> x0, local copies, waits for them, and re-layouts: 27 us -> none  [the longest x8 25.5 us: banded(): return jnp.tile(line, count)[:count * length].reshape(count, length)]
    concatenate x10 -> x0, local copies, waits for them, and re-layouts: 24 us -> none  [the longest x6 24 us: with_halo(): jnp.concatenate([lax.ppermute(tail, axis, [(i, (i + 1) % count) for i in...]
  transfers between devices with their start and end apart: 26 -> 0, of which waited for: 12 -> 0; matrix products, arithmetic and copies ran while one was open for 25% -> 0% of each run, Pallas kernels for 0% -> 0%
where the time goes in v1:
time: 119 us; the launch traced here: 117 us
  Pallas kernels  113 us (95%)
  local copies, waits for them, and re-layouts  3.73 us (3%)
    pallas_call x1, Pallas kernels, sweeps(): pl.pallas_call(functools.partial(sweep_kernel, n_row, n_col), in_specs=[a...  65.3 us
    pallas_call x1, Pallas kernels, energy(): pl.pallas_call(functools.partial(energy_kernel, (rows, sub, width, unroll...  47.7 us
    unnamed x10, local copies, waits for them, and re-layouts  3.73 us

profile of v1, /device:TPU:24, one launch (start us, length us, event | category | flops | bytes accessed | tf_op | source)
XLA Modules:
  0.0 117.4 jit_solution(9621816389322389747)
XLA Ops:
  0.6 0.0 copy-start
  0.6 0.0 copy-start.1
  0.7 1.7 %copy-done.1 = f32[512,1024]{1,0:T(8,128)S(1)} copy-done((f32[512,1024]{1,0:T(8,128)S(1)}, f32[512,1024]{1,0:T(8,128)}, u32[]{:S(2)}) %copy-start.1) | copy-done | bytes 2097176
  2.4 0.0 copy-start.2
  2.4 0.7 copy-done.2
  3.1 0.0 copy-start.3
  3.1 0.7 copy-done.3
  3.7 0.0 copy-start.4
  3.7 0.7 copy-done.4
  4.4 65.3 %sweeps.1 = (f32[512,1024]{1,0:T(8,128)S(1)}, bf16[16,528,128]{2,1,0:T(8,128)(2,1)}, s32[1,128]{1,0:T(1,128)S(1)}) custom-call(f32[31]{0:T(128)S(1)} %copy-done.3, f32[31]{0:T(128)S(1)} %copy-done.4, s32[4,8]{1,0:T(4,128)S(1)} %copy-done.2, f32[512,1024]{1,0:T(8,128)S(1)} %copy-done.1, bf16[2,512,1024]{2,1,0:T(8,128)(2,1)} %sentinel.1), custom_call_target="tpu_custom_call" | custom-call | tf_op jit(solution)/shard_map/sweeps/pallas_call | solution.py:449
  69.7 0.0 copy-done
  69.7 47.7 %energy.1 = (f32[512,1024]{1,0:T(8,128)}, f32[512,1024]{1,0:T(8,128)}, f32[512,1024]{1,0:T(8,128)}) custom-call(s32[1,128]{1,0:T(1,128)S(1)} %get-tuple-element.6.place, bf16[16,528,128]{2,1,0:T(8,128)(2,1)} %get-tuple-element.7.arrived, f32[512,1024]{1,0:T(8,128)S(1)} %get-tuple-element.8.theta, f32[512,1024]{1,0:T(8,128)S(1)} %copy-done, ...), custom_call_target="tpu_custom_call" | custom-call | tf_op jit(solution)/shard_map/energy/pallas_call | solution.py:133
Async XLA Ops:
  0.6 69.1 %copy-start = (f32[512,1024]{1,0:T(8,128)S(1)}, f32[512,1024]{1,0:T(8,128)}, u32[]{:S(2)}) copy-start(f32[512,1024]{1,0:T(8,128)} %air.1) | copy-start | bytes 6291460
  0.6 1.7 %copy-start.1 = (f32[512,1024]{1,0:T(8,128)S(1)}, f32[512,1024]{1,0:T(8,128)}, u32[]{:S(2)}) copy-start(f32[512,1024]{1,0:T(8,128)} %observed.1) | copy-start | bytes 6291460
  2.4 0.7 copy-start.2
  3.1 0.7 copy-start.3
  3.7 0.7 copy-start.4

commit v2 on v1

--- a/solution.py
+++ b/solution.py
@@ -314,18 +314,30 @@
     row_b[:TALL, :], row_b[TALL:2 * TALL, :], row_b[2 * TALL:, :] = split(first[:TALL, :])
     starts = (-64, -32, 0, 416, 352, 384)
     for n, start in enumerate((None, *starts)):
-        left = first[:TALL, :]
-        if start is not None:
-            left = jnp.where(inside((TALL, WINDOW), 1, row0 + (start - FRAME // 3), scene_rows), left, 0.0)
-        row_g[n, :TALL, :], row_g[n, TALL:2 * TALL, :], row_g[n, 2 * TALL:, :] = split(precise(left, second[...]))
+        def make_rows(n=n, start=start):
+            left = first[:TALL, :]
+            if start is not None:
+                left = jnp.where(inside((TALL, WINDOW), 1, row0 + (start - FRAME // 3), scene_rows), left, 0.0)
+            row_g[n, :TALL, :], row_g[n, TALL:2 * TALL, :], row_g[n, 2 * TALL:, :] = split(precise(left, second[...]))
+
+        if start is None:
+            make_rows()
+        else:
+            pl.when(row == (0 if n < 4 else n_row - 1))(make_rows)
     taps_matrix(first, kcol, WINDOW, BLOCK, half + SPAN, -1)
     taps_matrix(second, kcol, WINDOW, WINDOW, SPAN, 1)
     col_b[:, :BLOCK], col_b[:, BLOCK:2 * BLOCK], col_b[:, 2 * BLOCK:] = split(first[:, :BLOCK])
     for n, start in enumerate((None, 0, tile_cols - BLOCK)):
-        right = first[:, :BLOCK]
-        if start is not None:
-            right = jnp.where(inside((WINDOW, BLOCK), 0, col0 + (start - half), scene_cols), right, 0.0)
-        col_g[n, :, :BLOCK], col_g[n, :, BLOCK:2 * BLOCK], col_g[n, :, 2 * BLOCK:] = split(precise(second[...], right))
+        def make_cols(n=n, start=start):
+            right = first[:, :BLOCK]
+            if start is not None:
+                right = jnp.where(inside((WINDOW, BLOCK), 0, col0 + (start - half), scene_cols), right, 0.0)
+            col_g[n, :, :BLOCK], col_g[n, :, BLOCK:2 * BLOCK], col_g[n, :, 2 * BLOCK:] = split(precise(second[...], right))
+
+        if start is None:
+            make_cols()
+        else:
+            pl.when(col == (0 if n == 1 else n_col - 1))(make_cols)
     for ref in (mid, midb):
         for n in range(3):
             ref[n, pl.ds(rows, 32), :] = jnp.zeros((32, cols), jnp.bfloat16)
@@ -363,7 +375,7 @@
         def block(j, carry):
             at = pl.ds(pl.multiple_of(j * BLOCK, BLOCK), WINDOW)
             put = (pl.ds(0, height), pl.ds(pl.multiple_of(j * BLOCK, BLOCK), BLOCK))
-            kind = jnp.where(j == 1, 1, jnp.where(j == per_c, 2, 0))
+            kind = jnp.where((j == 1) & (col == 0), 1, jnp.where((j == per_c) & (col == n_col - 1), 2, 0))
             x1, x2, x3 = (flat[q, pl.ds(0, height), at] for q in range(3))
 
             def apply(weights, to):
@@ -392,7 +404,8 @@
             def strip(n, carry, offset=offset, size=size, kind=kind):
                 across = pl.ds(pl.multiple_of(n * WINDOW, WINDOW) + begin, WINDOW)
                 at = (pl.ds(offset, WINDOW), across)
-                blurred = along_rows(row_g[kind], mid, at, size)
+                chosen = jnp.where(row == (0 if kind < 4 else n_row - 1), kind, 0)
+                blurred = along_rows(row_g[chosen], mid, at, size)
                 if start == -64:
                     extra = along_rows(row_b[...], midb, at, size)
                     nudge[pl.ds(offset, size), across] = extra

time: 119 us -> 119 us (level)
  no operation moved by 1% of the time
where the time goes in v2:
time: 119 us; the launch traced here: 117 us
  Pallas kernels  113 us (95%)
  local copies, waits for them, and re-layouts  3.73 us (3%)
    pallas_call x1, Pallas kernels, sweeps(): pl.pallas_call(functools.partial(sweep_kernel, n_row, n_col), in_specs=[a...  65.3 us
    pallas_call x1, Pallas kernels, energy(): pl.pallas_call(functools.partial(energy_kernel, (rows, sub, width, unroll...  47.7 us
    unnamed x10, local copies, waits for them, and re-layouts  3.73 us

profile of v2, /device:TPU:24, one launch (start us, length us, event | category | flops | bytes accessed | tf_op | source)
XLA Modules:
  0.0 117.4 jit_solution(13038404783026028326)
XLA Ops:
  0.6 0.0 copy-start
  0.6 0.0 copy-start.1
  0.7 1.7 %copy-done.1 = f32[512,1024]{1,0:T(8,128)S(1)} copy-done((f32[512,1024]{1,0:T(8,128)S(1)}, f32[512,1024]{1,0:T(8,128)}, u32[]{:S(2)}) %copy-start.1) | copy-done | bytes 2097176
  2.4 0.0 copy-start.2
  2.4 0.7 copy-done.2
  3.1 0.0 copy-start.3
  3.1 0.7 copy-done.3
  3.7 0.0 copy-start.4
  3.7 0.7 copy-done.4
  4.4 65.3 %sweeps.1 = (f32[512,1024]{1,0:T(8,128)S(1)}, bf16[16,528,128]{2,1,0:T(8,128)(2,1)}, s32[1,128]{1,0:T(1,128)S(1)}) custom-call(f32[31]{0:T(128)S(1)} %copy-done.3, f32[31]{0:T(128)S(1)} %copy-done.4, s32[4,8]{1,0:T(4,128)S(1)} %copy-done.2, f32[512,1024]{1,0:T(8,128)S(1)} %copy-done.1, bf16[2,512,1024]{2,1,0:T(8,128)(2,1)} %sentinel.1), custom_call_target="tpu_custom_call" | custom-call | tf_op jit(solution)/shard_map/sweeps/pallas_call | solution.py:462
  69.7 0.0 copy-done
  69.7 47.7 %energy.1 = (f32[512,1024]{1,0:T(8,128)}, f32[512,1024]{1,0:T(8,128)}, f32[512,1024]{1,0:T(8,128)}) custom-call(s32[1,128]{1,0:T(1,128)S(1)} %get-tuple-element.6.place, bf16[16,528,128]{2,1,0:T(8,128)(2,1)} %get-tuple-element.7.arrived, f32[512,1024]{1,0:T(8,128)S(1)} %get-tuple-element.8.theta, f32[512,1024]{1,0:T(8,128)S(1)} %copy-done, ...), custom_call_target="tpu_custom_call" | custom-call | tf_op jit(solution)/shard_map/energy/pallas_call | solution.py:133
Async XLA Ops:
  0.6 69.0 %copy-start = (f32[512,1024]{1,0:T(8,128)S(1)}, f32[512,1024]{1,0:T(8,128)}, u32[]{:S(2)}) copy-start(f32[512,1024]{1,0:T(8,128)} %air.1) | copy-start | bytes 6291460
  0.6 1.7 %copy-start.1 = (f32[512,1024]{1,0:T(8,128)S(1)}, f32[512,1024]{1,0:T(8,128)}, u32[]{:S(2)}) copy-start(f32[512,1024]{1,0:T(8,128)} %observed.1) | copy-start | bytes 6291460
  2.4 0.7 copy-start.2
  3.1 0.7 copy-start.3
  3.7 0.7 copy-start.4
